TPU v7x, 32 devices: a whole 2x2x4 slice. The times are simulated.
32 devices in a mesh: poles: 2 (over x), row: 8 (over z, y), col: 2 (over core).
Axes of the slice: x: 2, y: 2, z: 4, core: 2. Of those that a mesh axis runs over, the one named last changes fastest.
Arguments:
- root_inverse: bfloat16 [16384, 8192], P(('poles', 'row'), 'col'), parts along dimension 0, may hold values from -6 to 6
- panels: bfloat16 [4, 1024, 8192], P(('poles', 'col'), None, 'row'), parts along dimension 0, may hold values from -0.1875 to 0.1875
- diag_inverse: bfloat16 [4, 8192, 8192], P(('poles', 'col'), 'row'), parts along dimension 0, may hold values from -6 to 6
- row_lists: int32 [2, 1024], replicated, may hold values from 0 to 8191, as said below
Outputs:
- offdiag_inverse: bfloat16 [4, 1024, 8192], P(('poles', 'col'), None, 'row'), parts along dimension 0
- diag_result: bfloat16 [4, 8192, 8192], P(('poles', 'col'), 'row'), parts along dimension 0
There are 2 independent parts, one for each index of `poles`. A program takes and returns all parts, laid end to end along the dimension named above; an argument that names none is the same for every part. Nothing has to cross between parts.
Inputs may be any that keep to these rules, and one draw needn't show every extreme that they name: `row_lists`: each child's list is strictly increasing and holds the first and the last root row. In each aligned run of 1024 root rows at most 256 of one child's indices fall, and exactly 256 in one run of every list.
All inputs are finite; a program needn't handle non-finite values.
Results may differ from a plain program's by a relative error of at most 0.0055.
Values may be sent and summed in bfloat16 or wider, within the bound.
A program may use at most 192 MiB of HBM per device.

v0:
```python
import jax
import jax.numpy as jnp
from jax import lax
from jax.sharding import PartitionSpec as P


def pick_listed(root_block, rows, row_index, col_index, most):
    block_rows = root_block.shape[0]
    half_cols = root_block.shape[1]
    listed = rows.shape[0]
    lower = row_index * block_rows
    first = jnp.sum((rows < lower).astype(jnp.int32))
    count = jnp.sum(((rows >= lower) & (rows < lower + block_rows)).astype(jnp.int32))
    offsets = jnp.arange(most, dtype=jnp.int32)
    positions = jnp.clip(first + offsets, 0, listed - 1)
    local_rows = jnp.clip(jnp.take(rows, positions) - lower, 0, block_rows - 1)
    taken = jnp.take(root_block, local_rows, axis=0)
    local_cols = rows - col_index * half_cols
    col_valid = (local_cols >= 0) & (local_cols < half_cols)
    picked = jnp.take(taken, jnp.clip(local_cols, 0, half_cols - 1), axis=1)
    valid = (offsets < count)[:, None] & col_valid[None, :]
    return (jnp.where(valid, picked, jnp.zeros_like(picked)), first, count)


def per_device(root_inverse, panels, diag_inverse, row_lists):
    row_index = lax.axis_index("row")
    col_index = lax.axis_index("col")
    n_rows = lax.axis_size("row")
    listed = row_lists.shape[1]
    most = 2 * listed // n_rows
    block_rows = root_inverse.shape[0]
    first_pick, _, _ = pick_listed(root_inverse, row_lists[0], row_index, col_index, most)
    second_pick, _, _ = pick_listed(root_inverse, row_lists[1], row_index, col_index, most)
    both_picks = jnp.stack([first_pick, second_pick]).astype(jnp.float32)
    own_rows = (
        lax.psum_scatter(both_picks.astype(jnp.bfloat16), "col", scatter_dimension=0, tiled=True)
        .astype(jnp.float32)[0]
        .astype(jnp.bfloat16)
    )
    child_rows = lax.dynamic_index_in_dim(row_lists, col_index, 0, keepdims=False)
    gathered = lax.all_gather(own_rows, "row", axis=0, tiled=True)
    owners = child_rows // block_rows
    bounds = jnp.arange(n_rows, dtype=jnp.int32) * block_rows
    starts = jnp.sum((child_rows[None, :] < bounds[:, None]).astype(jnp.int32), axis=1)
    ranking = jnp.arange(listed, dtype=jnp.int32) - jnp.take(starts, owners)
    root_part = jnp.take(gathered, owners * most + ranking, axis=0)
    panel = panels[0]
    offdiag = (-jnp.dot(root_part, panel, preferred_element_type=jnp.float32)).astype(jnp.bfloat16)
    diag_rows = diag_inverse[0]
    update_rows = lax.dot_general(
        offdiag,
        lax.all_gather(panel, "row", axis=1, tiled=True),
        (((0,), (0,)), ((), ())),
        preferred_element_type=jnp.float32,
    )
    block_mine = (diag_rows.astype(jnp.float32) - update_rows).astype(jnp.bfloat16)
    partner = lax.all_to_all(block_mine, "row", split_axis=1, concat_axis=0, tiled=True)
    result = ((block_mine.astype(jnp.float32) + partner.T.astype(jnp.float32)) * 0.5).astype(
        jnp.bfloat16
    )
    return (offdiag[None], result[None])


def solution(mesh):
    placed = (
        P(("poles", "row"), "col"),
        P(("poles", "col"), None, "row"),
        P(("poles", "col"), "row", None),
        P(),
    )
    return jax.shard_map(
        per_device,
        mesh=mesh,
        in_specs=placed,
        out_specs=(P(("poles", "col"), None, "row"), P(("poles", "col"), "row", None)),
        check_vma=False,
    )
```

profile of v0, /device:TPU:12, one launch (start us, length us, event | category | flops | bytes accessed | tf_op | source)
XLA Modules:
  0.0 843.3 jit_solution(16834829791201554010)
XLA Ops:
  7.2 0.0 reduce-scatter.2.cloned.1.call-start
  7.2 0.8 and_reduce_fusion.1
  8.0 0.8 constant_dynamic-slice_fusion
  8.9 0.8 convert_reduce_fusion.2
  9.6 0.6 iota_compare_fusion
  10.3 0.6 iota_compare_fusion.1
  10.9 0.7 compare_select_fusion.16
  11.5 0.7 compare_select_fusion.18
  12.2 1.4 gather_fusion.1
  13.6 0.7 compare_and_fusion.4
  14.3 1.4 gather_fusion.4
  15.7 0.7 compare_and_fusion.3
  16.4 8.3 gather_fusion.2
  24.8 1.6 broadcast_select_fusion.1
  26.3 3.3 copy.19
  29.6 9.7 %gather_fusion.5 = bf16[256,4096]{1,0:T(8,128)(2,1)} fusion(bf16[1024,4096]{1,0:T(8,128)(2,1)} %param.10, s32[1024]{0:T(1024)S(1)} %pad_clamp_fusion), kind=kCustom, calls=%fused_computation.4.clone | custom fusion | bytes 4195328 | tf_op jit(solution)/shard_map/jit(_take)/gather | solution.py:17
  39.3 3.2 broadcast_select_fusion
  42.4 4.1 copy.20
  46.5 3.9 gather_fusion.3
  50.4 5.5 gather_fusion.6
  56.0 0.3 fusion.9
  56.3 0.3 fusion.10
  56.7 1.1 pad_maximum_fusion
  57.7 0.0 reduce-scatter.2.cloned.1.call-update
  57.7 0.0 all-gather.5.cloned.1.call-start
  57.8 10.0 %reduce-scatter.2.cloned.1.call-done = bf16[1,256,1024]{1,2,0:T(8,128)(2,1)} async-done(((bf16[2,256,1024]{1,2,0:T(8,128)(2,1)}), bf16[1,256,1024]{1,2,0:T(8,128)(2,1)}) %reduce-scatter.2.cloned.1.call-update) | async-done | bytes 524304 | tf_op jit(solution)/shard_map/reduce_scatter | solution.py:36
  67.8 0.0 all-gather.5.cloned.1.call-update
  67.8 0.0 all-gather.7.cloned.1.call-start
  67.9 0.7 all-gather.7.cloned.1.call-update
  68.6 0.2 convert_reduce_fusion
  68.8 0.7 fusion.19
  69.4 4.3 compare_select_fusion.2
  73.8 0.7 compare_and_fusion.2
  74.5 68.6 %all-gather.5.cloned.1.call-done = bf16[1,2048,1024]{1,2,0:T(8,128)(2,1)} async-done(((bf16[1,256,1024]{1,2,0:T(8,128)(2,1)}), bf16[1,2048,1024]{1,2,0:T(8,128)(2,1)}) %all-gather.5.cloned.1.call-update) | async-done | bytes 4194320 | tf_op jit(solution)/shard_map/all_gather | solution.py:41
  143.2 6.4 copy.21
  149.5 7.7 gather_fusion
  157.3 5.5 negate_convert_fusion
  162.8 208.6 %all-gather.7.cloned.1.call-done = bf16[1,1024,8192]{2,1,0:T(8,128)(2,1)} async-done(((bf16[1,1024,1024]{2,1,0:T(8,128)(2,1)}), bf16[1,1024,8192]{2,1,0:T(8,128)(2,1)}) %all-gather.7.cloned.1.call-update) | async-done | bytes 16777232 | tf_op jit(solution)/shard_map/all_gather | solution.py:52
  371.4 26.1 %fusion = bf16[1024,8192]{1,0:T(8,128)(2,1)} fusion(bf16[1024,1024]{1,0:T(8,128)(2,1)} %negate_convert_fusion, bf16[1,1024,8192]{2,1,0:T(8,128)(2,1)} %param.12, bf16[1,1024,8192]{2,1,0:T(8,128)(2,1)} %all-gather.7.cloned.1.call-done), kind=kOutput, calls=%fused_computation.8 | convolution fusion | flops 17205035008 | bytes 52428800 | tf_op jit(solution)/shard_map/dot_general | solution.py:50
  397.5 8.1 copy.27
  405.6 366.7 %all_to_all.13 = bf16[1024,8,1024]{2,0,1:T(8,128)(2,1)S(1)} all-to-all(bf16[1024,8,1024]{2,0,1:T(8,128)(2,1)S(1)} %bitcast.67), channel_id=1, replica_groups=mesh['poles'=2,'row'=8,'col'=2] {'row'}, dimensions={1} | all-to-all | bytes 33554432 | tf_op jit(solution)/shard_map/all_to_all | solution.py:57
  772.3 11.2 %convert_element_type.71 = f32[1024,8,1024]{2,0,1:T(8,128)} convert(bf16[1024,8,1024]{2,0,1:T(8,128)(2,1)S(1)} %all_to_all.13) | non-fusion elementwise | flops 8388608 | bytes 50331648 | tf_op jit(solution)/shard_map/convert_element_type | solution.py:58
  783.6 31.1 %copy.24 = f32[8192,1024]{0,1:T(8,128)} copy(f32[8192,1024]{1,0:T(8,128)} %bitcast.66) | data formatting | bytes 67108864 | tf_op jit(solution)/shard_map/convert_element_type | solution.py:58
  814.6 22.1 %fusion.3 = bf16[1,1024,8192]{2,1,0:T(8,128)(2,1)} fusion(f32[8192,1024]{0,1:T(8,128)} %copy.24, bf16[1024,8192]{1,0:T(8,128)(2,1)} %fusion), kind=kLoop, calls=%fused_computation.12 | loop fusion | flops 33554432 | bytes 67108864 | tf_op jit(solution)/shard_map/broadcast_in_dim | solution.py:61
  (9 shorter events, 0.1 us)
Async XLA Ops:
  7.2 60.6 %reduce-scatter.2.cloned.1.call-start = ((), (), s32[]{:S(2)}) async-start(), calls=%async_computation.2 | async-start | bytes 1572864 | tf_op jit(solution)/shard_map/reduce_scatter | solution.py:36
  57.7 85.4 %all-gather.5.cloned.1.call-start = ((), (), s32[]{:S(2)}) async-start(), calls=%async_computation.3 | async-start | bytes 4718592 | tf_op jit(solution)/shard_map/all_gather | solution.py:41
  67.8 303.6 %all-gather.7.cloned.1.call-start = ((), (), s32[]{:S(2)}) async-start(), calls=%async_computation.4 | async-start | bytes 18874368 | tf_op jit(solution)/shard_map/all_gather | solution.py:52
Sparse Core Ops, SparseCore 0:
  57.9 9.8 reduce-scatter.1
  70.0 73.0 all-gather.4
  145.6 225.7 all-gather.6
where the time goes:
time: 848 us; the launch traced here: 843 us
  blocking collectives  367 us (43%)
  waiting for transfers between devices  288 us (34%)
  local copies, waits for them, and re-layouts  92.3 us (11%)
  other arithmetic  50.6 us (6%)
  matrix products  31.6 us (4%)
  between operations  13.9 us (2%)
    all_to_all x1, blocking collectives, per_device(): lax.all_to_all(block_mine, 'row', split_axis=1, concat_axis=0, tiled=True)  367 us
    all_gather x1, waiting for transfers between devices, per_device(): lax.all_gather(panel, 'row', axis=1, tiled=True)  209 us
    all_gather x1, waiting for transfers between devices, per_device(): gathered = lax.all_gather(own_rows, 'row', axis=0, tiled=True)  68.6 us
    convert_element_type x1, local copies, waits for them, and re-layouts, per_device(): partner.T.astype(jnp.float32)  31.1 us
    dot_general x1, matrix products, per_device(): lax.dot_general(offdiag, lax.all_gather(panel, 'row', axis=1, tiled=True)...  26.1 us
    broadcast_in_dim x1, other arithmetic, per_device(): return (offdiag[None], result[None])  22.1 us
    gather x2, local copies, waits for them, and re-layouts, pick_listed(): taken = jnp.take(root_block, local_rows, axis=0)  18 us
  transfers between devices with their start and end apart: 3, of which 3 were waited for; matrix products, arithmetic and copies ran while one was open for 3% of the time, Pallas kernels for 0%

commit v1 on v0

v1 whole, which is shorter than its diff:
```python
import functools

import jax
import jax.numpy as jnp
from jax import lax
from jax.experimental import pallas as pl
from jax.experimental.pallas import tpu as pltpu
from jax.sharding import PartitionSpec as P

MESH = pl.DeviceIdType.MESH
F32 = jnp.float32
BF16 = jnp.bfloat16


def flip(row, mask):
    bit = 1
    while bit <= mask:
        if mask & bit:
            row = row + bit - 2 * bit * ((row // bit) % 2)
        bit *= 2
    return row


def tile_of(size, most):
    return most if size % most == 0 else size


def exchange_kernel(
    n, root_ref, panel_ref, diag_ref, sel_ref, cols_ref, place_ref,
    off_ref, mine_ref, theirs_ref,
    root_v, picks, other_pick, listed, root_part, root_part_t, wide_t, p_all, d_buf,
    local_sem, copy_sem, x_sem, p_send, p_recv, g_send, g_recv, d_send, d_recv,
):
    half = n // 2
    row = lax.axis_index("row")
    col = lax.axis_index("col")
    side = row // half
    computes = (side + col) % 2 == 1
    keeps = (side + col) % 2 == 0
    block = panel_ref.shape[2]
    depth = panel_ref.shape[1]
    most = picks.shape[1]
    peers = [flip(row, m) for m in range(n)]

    def diag_block(m):
        start = pl.multiple_of(peers[m] * block, block)
        return diag_ref.at[0, :, pl.ds(start, block)]

    root_copy = pltpu.make_async_copy(root_ref, root_v, local_sem.at[0])
    root_copy.start()
    panel_copy = pltpu.make_async_copy(panel_ref.at[0], p_all.at[0], local_sem.at[1])
    panel_copy.start()
    own_copy = pltpu.make_async_copy(diag_block(0), theirs_ref.at[0], copy_sem.at[0])
    own_copy.start()

    barrier = pltpu.get_barrier_semaphore()
    for m in range(1, n):
        pl.semaphore_signal(barrier, inc=1, device_id={"row": peers[m]}, device_id_type=MESH)
    pl.semaphore_signal(barrier, inc=1, device_id={"col": 1 - col}, device_id_type=MESH)
    pl.semaphore_wait(barrier, n)

    def remote(src, dst, send, recv, mask):
        return pltpu.make_async_remote_copy(
            src_ref=src, dst_ref=dst, send_sem=send, recv_sem=recv,
            device_id={"row": peers[mask]}, device_id_type=MESH,
        )

    def spread(buf, send, recv, base):
        held, steps, bit = [base], [], half // 2
        while bit >= 1:
            steps.append([
                remote(buf.at[m], buf.at[m ^ bit], send.at[base + len(held) - 1 + i],
                       recv.at[m ^ bit], bit)
                for i, m in enumerate(held)
            ])
            held = held + [m ^ bit for m in held]
            bit //= 2
        return steps

    def cross(buf, send, recv):
        return remote(buf.at[0], buf.at[half], send.at[n - 1], recv.at[half], half)

    def send_diag(m):
        return remote(diag_block(m), theirs_ref.at[m], d_send.at[m], d_recv.at[m], m)

    def send_mine(m):
        return remote(mine_ref.at[m], theirs_ref.at[m], d_send.at[m], d_recv.at[m], m)

    p_own, p_far = spread(p_all, p_send, p_recv, 0), spread(p_all, p_send, p_recv, half)
    g_own, g_far = spread(listed, g_send, g_recv, 0), spread(listed, g_send, g_recv, half)
    p_cross, g_cross = cross(p_all, p_send, p_recv), cross(listed, g_send, g_recv)

    panel_copy.wait()

    @pl.when(keeps)
    def _():
        p_cross.start()

    if p_own:
        p_own[0][0].start()

    root_copy.wait()
    block_rows, half_cols = root_v.shape
    width = tile_of(half_cols, 512)
    row_ids = lax.broadcasted_iota(jnp.int32, (2 * most, block_rows), 1)
    take_rows = jnp.where(sel_ref[...] == row_ids, 1.0, 0.0).astype(BF16)

    def pick_tile(t, carry):
        own, far = carry
        at = pl.multiple_of(t * width, width)
        taken = jnp.dot(take_rows, root_v[:, pl.ds(at, width)], preferred_element_type=F32).astype(BF16)
        col_ids = lax.broadcasted_iota(jnp.int32, (width, depth), 0) + t * width
        take_own = jnp.where(cols_ref[0:1, :] == col_ids, 1.0, 0.0).astype(BF16)
        take_far = jnp.where(cols_ref[1:2, :] == col_ids, 1.0, 0.0).astype(BF16)
        own = own + jnp.dot(taken[:most], take_own, preferred_element_type=F32)
        far = far + jnp.dot(taken[most:], take_far, preferred_element_type=F32)
        return own, far

    zero = jnp.zeros((most, depth), F32)
    own, far = lax.fori_loop(0, half_cols // width, pick_tile, (zero, zero))
    picks[1] = far.astype(BF16)
    picks[0] = own.astype(BF16)
    over = pltpu.make_async_remote_copy(
        src_ref=picks.at[1], dst_ref=other_pick, send_sem=x_sem.at[0], recv_sem=x_sem.at[1],
        device_id={"col": 1 - col}, device_id_type=MESH,
    )
    over.start()
    over.wait()
    listed[0] = (picks[0].astype(F32) + other_pick[...].astype(F32)).astype(BF16)
    g_cross.start()
    if g_own:
        g_own[0][0].start()

    @pl.when(keeps)
    def _():
        for m in range(half, n):
            send_diag(m).start()
        for m in range(half, n):
            pltpu.make_async_copy(diag_block(m), mine_ref.at[m], copy_sem.at[m]).start()

    @pl.when(computes)
    def _():
        for m in range(1, half):
            send_diag(m).start()

    def finish(steps, k):
        for copy in steps[k]:
            copy.wait_recv()

    def begin(steps, k):
        if k < len(steps):
            for copy in steps[k]:
                copy.start()

    levels = len(p_own)
    for k in range(levels):
        finish(g_own, k)
        begin(g_own, k + 1)
        if k == 0:
            g_cross.wait_recv()
        else:
            finish(g_far, k - 1)
        begin(g_far, k)
        finish(p_own, k)
        begin(p_own, k + 1)

        @pl.when(computes)
        def _():
            if k == 0:
                p_cross.wait_recv()
            else:
                finish(p_far, k - 1)
            begin(p_far, k)

    if levels:
        finish(g_far, levels - 1)
    else:
        g_cross.wait_recv()

        @pl.when(computes)
        def _():
            p_cross.wait_recv()

    @pl.when(keeps)
    def _():
        for m in range(1, half):
            send_diag(m).start()

    rows_step = tile_of(depth, 256)
    slots = listed.shape[0] * most
    all_listed = listed[...].reshape(slots, depth)

    def put_rows(t, carry):
        at = pl.multiple_of(t * rows_step, rows_step)
        ids = lax.broadcasted_iota(jnp.int32, (rows_step, slots), 1)
        put = jnp.where(place_ref[pl.ds(at, rows_step), :] == ids, 1.0, 0.0).astype(BF16)
        root_part[pl.ds(at, rows_step), :] = jnp.dot(put, all_listed, preferred_element_type=F32).astype(BF16)
        return carry

    lax.fori_loop(0, depth // rows_step, put_rows, 0)

    def turn(t, carry):
        at = pl.multiple_of(t * rows_step, rows_step)
        root_part_t[:, pl.ds(at, rows_step)] = root_part[pl.ds(at, rows_step), :].astype(F32).T.astype(BF16)
        return carry

    lax.fori_loop(0, depth // rows_step, turn, 0)
    cols_step = tile_of(block, 256)

    def products(t, carry):
        at = pl.multiple_of(t * cols_step, cols_step)
        panel = p_all[0, :, pl.ds(at, cols_step)]
        plain = jnp.dot(root_part[...], panel, preferred_element_type=F32)
        turned = jnp.dot(root_part_t[...], panel, preferred_element_type=F32)
        off_ref[0, :, pl.ds(at, cols_step)] = (-plain).astype(BF16)
        wide_t[pl.ds(at, cols_step), :] = (plain + turned).T.astype(BF16)
        return carry

    lax.fori_loop(0, block // cols_step, products, 0)

    def update(m):
        load = pltpu.make_async_copy(diag_block(m), d_buf, local_sem.at[0])
        load.start()
        load.wait()

        def one(t, carry):
            at = pl.multiple_of(t * cols_step, cols_step)
            part = jnp.dot(wide_t[pl.ds(at, cols_step), :], p_all[m], preferred_element_type=F32)
            d_buf[pl.ds(at, cols_step), :] = (d_buf[pl.ds(at, cols_step), :].astype(F32) + part).astype(BF16)
            return carry

        lax.fori_loop(0, block // cols_step, one, 0)
        store = pltpu.make_async_copy(d_buf, mine_ref.at[m], local_sem.at[1])
        store.start()
        store.wait()

    @pl.when(computes)
    def _():
        for m in range(half, n):
            if levels and m == half + 1:
                finish(p_far, levels - 1)
            update(m)
            send_mine(m).start()

    for m in range(half):
        update(m)

    own_copy.wait()

    @pl.when(keeps)
    def _():
        p_cross.wait_send()
        for m in range(half, n):
            pltpu.make_async_copy(diag_block(m), mine_ref.at[m], copy_sem.at[m]).wait()
            send_diag(m).wait()

    @pl.when(computes)
    def _():
        for step in p_far:
            for copy in step:
                copy.wait_send()
        for m in range(half, n):
            send_mine(m).wait()

    g_cross.wait_send()
    for steps in (p_own, g_own, g_far):
        for step in steps:
            for copy in step:
                copy.wait_send()
    for m in range(1, half):
        send_diag(m).wait()


def symmetrize_kernel(row_ref, mine_ref, theirs_ref, out_ref):
    out_ref[0] = ((mine_ref[0].astype(F32) + theirs_ref[0].astype(F32).T) * 0.5).astype(BF16)


def per_device(root_inverse, panels, diag_inverse, row_lists):
    row = lax.axis_index("row")
    col = lax.axis_index("col")
    n = lax.axis_size("row")
    listed = row_lists.shape[1]
    most = 2 * listed // n
    block_rows, half_cols = root_inverse.shape
    block = panels.shape[2]

    own_rows = jnp.where(col == 0, row_lists[0], row_lists[1])
    far_rows = jnp.where(col == 0, row_lists[1], row_lists[0])
    both = jnp.stack([own_rows, far_rows])
    lower = row * block_rows
    inside = (both >= lower) & (both < lower + block_rows)
    spot = jnp.arange(listed, dtype=jnp.int32)
    first = jnp.sum((both < lower).astype(jnp.int32), axis=1, keepdims=True)
    rank = jnp.where(inside, spot[None] - first, -1)
    slots = jnp.arange(most, dtype=jnp.int32)
    hit = rank[:, None, :] == slots[None, :, None]
    sel = jnp.max(jnp.where(hit, both[:, None, :] - lower, -1), axis=2).reshape(2 * most, 1)
    cols = both - col * half_cols
    owner = own_rows // block_rows
    start = jnp.sum((own_rows[None, :] < (owner * block_rows)[:, None]).astype(jnp.int32), axis=1)
    place = (jnp.bitwise_xor(owner, row) * most + spot - start).reshape(listed, 1)

    hbm = pl.BlockSpec(memory_space=pl.ANY)
    vmem = pl.BlockSpec(memory_space=pltpu.VMEM)
    dma = pltpu.SemaphoreType.DMA
    off, mine, theirs = pl.pallas_call(
        functools.partial(exchange_kernel, n),
        out_shape=(
            jax.ShapeDtypeStruct(panels.shape, BF16),
            jax.ShapeDtypeStruct((n, block, block), BF16),
            jax.ShapeDtypeStruct((n, block, block), BF16),
        ),
        in_specs=[hbm, hbm, hbm, vmem, vmem, vmem],
        out_specs=(vmem, hbm, hbm),
        scratch_shapes=[
            pltpu.VMEM((block_rows, half_cols), BF16),
            pltpu.VMEM((2, most, listed), BF16),
            pltpu.VMEM((most, listed), BF16),
            pltpu.VMEM((n, most, listed), BF16),
            pltpu.VMEM((listed, listed), BF16),
            pltpu.VMEM((listed, listed), BF16),
            pltpu.VMEM((block, listed), BF16),
            pltpu.VMEM((n, listed, block), BF16),
            pltpu.VMEM((block, block), BF16),
            dma((2,)), dma((n,)), dma((2,)),
            dma((n,)), dma((n,)), dma((n,)), dma((n,)), dma((n,)), dma((n,)),
        ],
        compiler_params=pltpu.CompilerParams(
            collective_id=0, has_side_effects=True, vmem_limit_bytes=60 * 2**20
        ),
        name="exchange",
    )(root_inverse, panels, diag_inverse, sel, cols, place)

    strip = tile_of(block, 256)
    result = pl.pallas_call(
        symmetrize_kernel,
        grid_spec=pltpu.PrefetchScalarGridSpec(
            num_scalar_prefetch=1,
            grid=(n, block // strip),
            in_specs=[
                pl.BlockSpec((1, strip, block), lambda m, t, at: (m, t, 0)),
                pl.BlockSpec((1, block, strip), lambda m, t, at: (m, 0, t)),
            ],
            out_specs=pl.BlockSpec((1, strip, block), lambda m, t, at: (0, t, m ^ at[0])),
        ),
        out_shape=jax.ShapeDtypeStruct(diag_inverse.shape, BF16),
        compiler_params=pltpu.CompilerParams(vmem_limit_bytes=32 * 2**20),
        name="symmetrize",
    )(row.reshape(1), mine, theirs)
    return (off, result)


def solution(mesh):
    placed = (
        P(("poles", "row"), "col"),
        P(("poles", "col"), None, "row"),
        P(("poles", "col"), "row", None),
        P(),
    )
    return jax.shard_map(
        per_device,
        mesh=mesh,
        in_specs=placed,
        out_specs=(P(("poles", "col"), None, "row"), P(("poles", "col"), "row", None)),
        check_vma=False,
    )
```

time: 848 us -> 576 us (0.68)
  Pallas kernels: 0 us -> 562 us
  blocking collectives: 367 us -> 0 us
  waiting for transfers between devices: 288 us -> 0 us
  local copies, waits for them, and re-layouts: 92.3 us -> 8.4 us
  other arithmetic: 50.6 us -> 3.61 us
  matrix products: 31.6 us -> 0 us
  between operations: 13.9 us -> 0.68 us
    pallas_call x0 -> x2, Pallas kernels: none -> 562 us  [the longest x1 537 us: per_device(): pl.pallas_call(functools.partial(exchange_kernel, n), out_shape=(jax.Shap...]
    all_to_all x1 -> x0, blocking collectives: 367 us -> none  [per_device(): lax.all_to_all(block_mine, 'row', split_axis=1, concat_axis=0, tiled=True)]
    all_gather x2 -> x0, waiting for transfers between devices: 277 us -> none  [the longest x1 209 us: per_device(): lax.all_gather(panel, 'row', axis=1, tiled=True)]
    gather x8 -> x0, local copies, waits for them, and re-layouts: 38.6 us -> none  [the longest x2 18 us: pick_listed(): taken = jnp.take(root_block, local_rows, axis=0)]
    dot_general x2 -> x0, matrix products: 31.6 us -> none  [the longest x1 26.1 us: per_device(): lax.dot_general(offdiag, lax.all_gather(panel, 'row', axis=1, tiled=True)...]
    convert_element_type x1 -> x0, local copies, waits for them, and re-layouts: 31.1 us -> none  [per_device(): partner.T.astype(jnp.float32)]
    broadcast_in_dim x1 -> x0, other arithmetic: 22.1 us -> none  [per_device(): return (offdiag[None], result[None])]
    convert_element_type x1 -> x0, other arithmetic: 11.2 us -> none  [per_device(): partner.T.astype(jnp.float32)]
  transfers between devices with their start and end apart: 3 -> 0, of which waited for: 3 -> 0; matrix products, arithmetic and copies ran while one was open for 3% -> 0% of each run, Pallas kernels for 0% -> 0%
where the time goes in v1:
time: 576 us; the launch traced here: 575 us
  Pallas kernels  562 us (98%)
  local copies, waits for them, and re-layouts  8.4 us (1%)
    pallas_call x1, Pallas kernels, per_device(): pl.pallas_call(functools.partial(exchange_kernel, n), out_shape=(jax.Shap...  537 us
    pallas_call x1, Pallas kernels, per_device(): pl.pallas_call(symmetrize_kernel, grid_spec=pltpu.PrefetchScalarGridSpec(...  25.4 us

profile of v1, /device:TPU:12, one launch (start us, length us, event | category | flops | bytes accessed | tf_op | source)
XLA Modules:
  0.0 575.1 jit_solution(17006850002837210281)
XLA Ops:
  0.6 0.8 broadcast_select_fusion.1
  1.4 0.1 fusion.6
  1.6 0.6 convert_reduce_fusion
  2.1 0.6 broadcast_subtract_fusion
  2.7 0.3 select_reduce_fusion
  3.1 0.9 copy.28
  4.0 0.2 copy.23
  4.2 0.2 copy.18
  4.4 1.2 fusion.4.place_ref
  5.6 537.0 %exchange.1 = (bf16[1,1024,1024]{2,1,0:T(8,128)(2,1)}, bf16[8,1024,1024]{2,1,0:T(8,128)(2,1)}, bf16[8,1024,1024]{2,1,0:T(8,128)(2,1)}) custom-call(bf16[1024,4096]{1,0:T(8,128)(2,1)} %root_ref.1, bf16[1,1024,1024]{2,1,0:T(8,128)(2,1)} %panel_ref.1, bf16[1,1024,8192]{2,1,0:T(8,128)(2,1)} %diag_ref.1, s32[512,1]{1,0:T(8,128)} %bitcast.8, ...), custom_call_target="tpu_custom_call" | custom-call | tf_op jit(solution)/shard_map/exchange/pallas_call | solution.py:306
  542.6 0.0 copy-start
  542.6 5.8 %copy-done = bf16[8,1024,1024]{2,1,0:T(8,128)(2,1)S(1)} copy-done((bf16[8,1024,1024]{2,1,0:T(8,128)(2,1)S(1)}, bf16[8,1024,1024]{2,1,0:T(8,128)(2,1)}, u32[]{:S(2)}) %copy-start) | copy-done | bytes 16777240
  548.4 0.0 copy-start.1
  548.4 25.4 %symmetrize.1 = bf16[1,1024,8192]{2,1,0:T(8,128)(2,1)} custom-call(s32[1]{0:T(128)} %bitcast.3.row_ref, bf16[8,1024,1024]{2,1,0:T(8,128)(2,1)S(1)} %copy-done, bf16[8,1024,1024]{2,1,0:T(8,128)(2,1)} %get-tuple-element.7.theirs_ref), custom_call_target="tpu_custom_call" | custom-call | tf_op jit(solution)/shard_map/symmetrize/pallas_call | solution.py:335
  573.8 0.0 copy-done.1
  573.8 1.3 copy.30
  (2 shorter events, 0.0 us)
Async XLA Ops:
  542.6 5.8 %copy-start = (bf16[8,1024,1024]{2,1,0:T(8,128)(2,1)S(1)}, bf16[8,1024,1024]{2,1,0:T(8,128)(2,1)}, u32[]{:S(2)}) copy-start(bf16[8,1024,1024]{2,1,0:T(8,128)(2,1)} %get-tuple-element.6.mine_ref) | copy-start | bytes 50331652
  548.4 25.5 %copy-start.1 = (bf16[1,1024,1024]{2,1,0:T(8,128)(2,1)S(1)}, bf16[1,1024,1024]{2,1,0:T(8,128)(2,1)}, u32[]{:S(2)}) copy-start(bf16[1,1024,1024]{2,1,0:T(8,128)(2,1)} %get-tuple-element.15) | copy-start | bytes 6291460

commit v2 on v1

--- a/solution.py
+++ b/solution.py
@@ -65,39 +65,46 @@
             device_id={"row": peers[mask]}, device_id_type=MESH,
         )
 
-    def spread(buf, send, recv, base):
+    pieces = p_send.shape[1]
+    piece = depth // pieces
+
+    def panel_copy_to(source, slot, send, mask, c):
+        rows = pl.ds(c * piece, piece)
+        return remote(p_all.at[source, rows], p_all.at[slot, rows],
+                      p_send.at[send, c], p_recv.at[slot, c], mask)
+
+    def spread(base):
         held, steps, bit = [base], [], half // 2
         while bit >= 1:
             steps.append([
-                remote(buf.at[m], buf.at[m ^ bit], send.at[base + len(held) - 1 + i],
-                       recv.at[m ^ bit], bit)
-                for i, m in enumerate(held)
+                [panel_copy_to(m, m ^ bit, base + len(held) - 1 + i, bit, c) for i, m in enumerate(held)]
+                for c in range(pieces)
             ])
             held = held + [m ^ bit for m in held]
             bit //= 2
         return steps
 
-    def cross(buf, send, recv):
-        return remote(buf.at[0], buf.at[half], send.at[n - 1], recv.at[half], half)
-
     def send_diag(m):
         return remote(diag_block(m), theirs_ref.at[m], d_send.at[m], d_recv.at[m], m)
 
     def send_mine(m):
         return remote(mine_ref.at[m], theirs_ref.at[m], d_send.at[m], d_recv.at[m], m)
 
-    p_own, p_far = spread(p_all, p_send, p_recv, 0), spread(p_all, p_send, p_recv, half)
-    g_own, g_far = spread(listed, g_send, g_recv, 0), spread(listed, g_send, g_recv, half)
-    p_cross, g_cross = cross(p_all, p_send, p_recv), cross(listed, g_send, g_recv)
+    p_own, p_far = spread(0), spread(half)
+    p_cross = [panel_copy_to(0, half, n - 1, half, c) for c in range(pieces)]
+    g_cross = remote(listed.at[0], listed.at[half], g_send.at[half], g_recv.at[half], half)
+    g_own = [remote(listed.at[0], listed.at[m], g_send.at[m], g_recv.at[m], m) for m in range(1, half)]
+    g_far = [
+        remote(listed.at[half], listed.at[m], g_send.at[m], g_recv.at[m], m - half)
+        for m in range(half + 1, n)
+    ]
 
     panel_copy.wait()
 
     @pl.when(keeps)
     def _():
-        p_cross.start()
-
-    if p_own:
-        p_own[0][0].start()
+        for copy in p_cross:
+            copy.start()
 
     root_copy.wait()
     block_rows, half_cols = root_v.shape
@@ -128,8 +135,8 @@
     over.wait()
     listed[0] = (picks[0].astype(F32) + other_pick[...].astype(F32)).astype(BF16)
     g_cross.start()
-    if g_own:
-        g_own[0][0].start()
+    for copy in g_own:
+        copy.start()
 
     @pl.when(keeps)
     def _():
@@ -138,53 +145,37 @@
         for m in range(half, n):
             pltpu.make_async_copy(diag_block(m), mine_ref.at[m], copy_sem.at[m]).start()
 
+    def finish(steps, k, c):
+        for copy in steps[k][c]:
+            copy.wait_recv()
+
+    def begin(steps, k, c):
+        if k < len(steps):
+            for copy in steps[k][c]:
+                copy.start()
+
+    levels = len(p_own)
+    g_cross.wait_recv()
+    for copy in g_far:
+        copy.start()
+
     @pl.when(computes)
     def _():
-        for m in range(1, half):
-            send_diag(m).start()
-
-    def finish(steps, k):
-        for copy in steps[k]:
-            copy.wait_recv()
-
-    def begin(steps, k):
-        if k < len(steps):
-            for copy in steps[k]:
-                copy.start()
-
-    levels = len(p_own)
-    for k in range(levels):
-        finish(g_own, k)
-        begin(g_own, k + 1)
-        if k == 0:
-            g_cross.wait_recv()
-        else:
-            finish(g_far, k - 1)
-        begin(g_far, k)
-        finish(p_own, k)
-        begin(p_own, k + 1)
-
-        @pl.when(computes)
-        def _():
-            if k == 0:
-                p_cross.wait_recv()
-            else:
-                finish(p_far, k - 1)
-            begin(p_far, k)
-
-    if levels:
-        finish(g_far, levels - 1)
-    else:
-        g_cross.wait_recv()
-
-        @pl.when(computes)
-        def _():
-            p_cross.wait_recv()
-
-    @pl.when(keeps)
-    def _():
-        for m in range(1, half):
-            send_diag(m).start()
+        for c in range(pieces):
+            p_cross[c].wait_recv()
+            begin(p_far, 0, c)
+        for k in range(levels - 1):
+            for c in range(pieces):
+                finish(p_far, k, c)
+                begin(p_far, k + 1, c)
+
+    for copy in g_own + g_far:
+        copy.wait_recv()
+
+    for c in range(pieces):
+        begin(p_own, 0, c)
+    for m in range(1, half):
+        send_diag(m).start()
 
     rows_step = tile_of(depth, 256)
     slots = listed.shape[0] * most
@@ -236,20 +227,36 @@
 
     @pl.when(computes)
     def _():
-        for m in range(half, n):
-            if levels and m == half + 1:
-                finish(p_far, levels - 1)
+        update(half)
+        send_mine(half).start()
+        arrived = [half]
+        for k in range(levels):
+            if k == levels - 1:
+                for c in range(pieces):
+                    finish(p_far, k, c)
+            fresh = [m ^ (half >> (k + 1)) for m in arrived]
+            for m in fresh:
+                update(m)
+                send_mine(m).start()
+            arrived = arrived + fresh
+
+    update(0)
+    arrived = [0]
+    for k in range(levels):
+        for c in range(pieces):
+            finish(p_own, k, c)
+            begin(p_own, k + 1, c)
+        fresh = [m ^ (half >> (k + 1)) for m in arrived]
+        for m in fresh:
             update(m)
-            send_mine(m).start()
-
-    for m in range(half):
-        update(m)
+        arrived = arrived + fresh
 
     own_copy.wait()
 
     @pl.when(keeps)
     def _():
-        p_cross.wait_send()
+        for copy in p_cross:
+            copy.wait_send()
         for m in range(half, n):
             pltpu.make_async_copy(diag_block(m), mine_ref.at[m], copy_sem.at[m]).wait()
             send_diag(m).wait()
@@ -257,22 +264,24 @@
     @pl.when(computes)
     def _():
         for step in p_far:
-            for copy in step:
-                copy.wait_send()
+            for copies in step:
+                for copy in copies:
+                    copy.wait_send()
         for m in range(half, n):
             send_mine(m).wait()
 
-    g_cross.wait_send()
-    for steps in (p_own, g_own, g_far):
-        for step in steps:
-            for copy in step:
+    for copy in [g_cross] + g_own + g_far:
+        copy.wait_send()
+    for step in p_own:
+        for copies in step:
+            for copy in copies:
                 copy.wait_send()
     for m in range(1, half):
         send_diag(m).wait()
 
 
 def symmetrize_kernel(row_ref, mine_ref, theirs_ref, out_ref):
-    out_ref[0] = ((mine_ref[0].astype(F32) + theirs_ref[0].astype(F32).T) * 0.5).astype(BF16)
+    out_ref[0] = ((mine_ref[0].astype(F32) + theirs_ref[0].T.astype(F32)) * 0.5).astype(BF16)
 
 
 def per_device(root_inverse, panels, diag_inverse, row_lists):
@@ -323,7 +332,7 @@
             pltpu.VMEM((n, listed, block), BF16),
             pltpu.VMEM((block, block), BF16),
             dma((2,)), dma((n,)), dma((2,)),
-            dma((n,)), dma((n,)), dma((n,)), dma((n,)), dma((n,)), dma((n,)),
+            dma((n, 4)), dma((n, 4)), dma((n,)), dma((n,)), dma((n,)), dma((n,)),
         ],
         compiler_params=pltpu.CompilerParams(
             collective_id=0, has_side_effects=True, vmem_limit_bytes=60 * 2**20
@@ -331,7 +340,7 @@
         name="exchange",
     )(root_inverse, panels, diag_inverse, sel, cols, place)
 
-    strip = tile_of(block, 256)
+    strip = tile_of(block, 512)
     result = pl.pallas_call(
         symmetrize_kernel,
         grid_spec=pltpu.PrefetchScalarGridSpec(
@@ -344,7 +353,7 @@
             out_specs=pl.BlockSpec((1, strip, block), lambda m, t, at: (0, t, m ^ at[0])),
         ),
         out_shape=jax.ShapeDtypeStruct(diag_inverse.shape, BF16),
-        compiler_params=pltpu.CompilerParams(vmem_limit_bytes=32 * 2**20),
+        compiler_params=pltpu.CompilerParams(vmem_limit_bytes=60 * 2**20),
         name="symmetrize",
     )(row.reshape(1), mine, theirs)
     return (off, result)

time: 576 us -> 503 us (0.87)
  Pallas kernels: 562 us -> 495 us
  local copies, waits for them, and re-layouts: 8.4 us -> 2.63 us
    pallas_call x1, Pallas kernels: 537 us -> 472 us  [per_device(): pl.pallas_call(functools.partial(exchange_kernel, n), out_shape=(jax.Shap...]
    unnamed x7 -> x5, local copies, waits for them, and re-layouts: 7.95 us -> 2.19 us
where the time goes in v2:
time: 503 us; the launch traced here: 502 us
  Pallas kernels  495 us (98%)
    pallas_call x1, Pallas kernels, per_device(): pl.pallas_call(functools.partial(exchange_kernel, n), out_shape=(jax.Shap...  472 us
    pallas_call x1, Pallas kernels, per_device(): pl.pallas_call(symmetrize_kernel, grid_spec=pltpu.PrefetchScalarGridSpec(...  23.1 us

profile of v2, /device:TPU:12, one launch (start us, length us, event | category | flops | bytes accessed | tf_op | source)
XLA Modules:
  0.0 501.7 jit_solution(13933383552653966106)
XLA Ops:
  0.6 0.8 broadcast_select_fusion.1
  1.4 0.1 fusion.6
  1.6 0.6 convert_reduce_fusion
  2.1 0.6 broadcast_subtract_fusion
  2.7 0.3 select_reduce_fusion
  3.1 0.9 copy.28
  4.0 0.2 copy.23
  4.2 0.2 copy.18
  4.4 1.2 fusion.4.place_ref
  5.6 471.7 %exchange.1 = (bf16[1,1024,1024]{2,1,0:T(8,128)(2,1)}, bf16[8,1024,1024]{2,1,0:T(8,128)(2,1)}, bf16[8,1024,1024]{2,1,0:T(8,128)(2,1)}) custom-call(bf16[1024,4096]{1,0:T(8,128)(2,1)} %root_ref.1, bf16[1,1024,1024]{2,1,0:T(8,128)(2,1)} %panel_ref.1, bf16[1,1024,8192]{2,1,0:T(8,128)(2,1)} %diag_ref.1, s32[512,1]{1,0:T(8,128)} %bitcast.8, ...), custom_call_target="tpu_custom_call" | custom-call | tf_op jit(solution)/shard_map/exchange/pallas_call | solution.py:315
  477.3 0.0 copy-start
  477.3 23.1 %symmetrize.1 = bf16[1,1024,8192]{2,1,0:T(8,128)(2,1)} custom-call(s32[1]{0:T(128)} %bitcast.3.row_ref, bf16[8,1024,1024]{2,1,0:T(8,128)(2,1)} %get-tuple-element.6.mine_ref, bf16[8,1024,1024]{2,1,0:T(8,128)(2,1)} %get-tuple-element.7.theirs_ref), custom_call_target="tpu_custom_call" | custom-call | tf_op jit(solution)/shard_map/symmetrize/pallas_call | solution.py:344
  500.4 0.0 copy-done
  500.4 1.3 copy.30
  (2 shorter events, 0.0 us)
Async XLA Ops:
  477.3 23.1 %copy-start = (bf16[1,1024,1024]{2,1,0:T(8,128)(2,1)S(1)}, bf16[1,1024,1024]{2,1,0:T(8,128)(2,1)}, u32[]{:S(2)}) copy-start(bf16[1,1024,1024]{2,1,0:T(8,128)(2,1)} %get-tuple-element.15) | copy-start | bytes 6291460
